TPU v7x, 32 devices: a whole 2x2x4 slice. The times are simulated.
32 devices in a mesh: vox: 4 (over y, core), fas: 8 (over z, x).
Axes of the slice: x: 2, y: 2, z: 4, core: 2. Of those that a mesh axis runs over, the one named last changes fastest.
Arguments:
- signal: float32 [64, 6144], P('vox', 'fas'), may hold values from -6 to 6
- initial_weights: float32 [262144], P('fas'), may hold values from 0.1 to 2
- coefficients: bfloat16 [8192, 4096], P(('vox', 'fas')), may hold values from 0 to 0.032958984
- block_rows: int32 [8192], P(('vox', 'fas')), may hold values from 0 to 63, as said below
- block_cols: int32 [8192], P(('vox', 'fas')), may hold values from 0 to 4095, as said below
- block_atoms: int32 [8192, 64], P(('vox', 'fas')), may hold values from 0 to 359
- block_count: int32 [32], P(('vox', 'fas')), may hold values from 64 to 256, as said below
- dictionary: bfloat16 [360, 96], replicated, may hold values from -6 to 6
Outputs:
- weights: float32 [262144], P('fas')
- residual: float32 [64, 6144], P('vox', 'fas')
Inputs may be any that keep to these rules, and one draw needn't show every extreme that they name: Block slots are stored device by device: the device with vox index i and fas index f holds slots (i * 8 + f) * 256 to (i * 8 + f + 1) * 256 - 1, and every block_rows value there lies in i * 16 to (i + 1) * 16 - 1. For the slots of the device with fas index f, every block_cols value lies in f * 512 to (f + 1) * 512 - 1. `block_count`: entry i * 8 + f is the number of live slots of the device with vox index i and fas index f, its first slots; some device has all 256 live.
All inputs are finite; a program needn't handle non-finite values.
Results may differ from a plain program's by a relative error of at most 0.0003.
Values sent between devices are 32-bit elements; how exact they have to be, the bound alone decides.
No kernel may reach another device: no remote copies, remote signals or barrier semaphores. Data moves between devices by JAX's collectives and lax.ppermute only.
A program may use at most 128 MiB of HBM per device.

v0:
```python
import jax
import jax.numpy as jnp
from jax import lax
from jax.sharding import PartitionSpec as P

BV = 64
BF = 64
DIRS = 96
ITERS = 5


def local(
    signal,
    initial_weights,
    coefficients,
    block_rows,
    block_cols,
    block_atoms,
    block_count,
    dictionary,
):
    vox_rows = signal.shape[0]
    fas_rows = initial_weights.shape[0] // BF
    slot_total = coefficients.shape[0]
    row_width = BV * DIRS
    fas_place = lax.axis_index("fas")
    rows_local = block_rows - lax.axis_index("vox") * vox_rows
    cols_local = block_cols - fas_place * fas_rows
    live_count = block_count[0]
    atom_table = dictionary[block_atoms]
    coef_view = coefficients.reshape(slot_total, BV, BF)
    group_size = min(256, slot_total)
    group_turns = (live_count + group_size - 1) // group_size
    vox_range = jnp.arange(vox_rows, dtype=jnp.int32)
    fas_range = jnp.arange(fas_rows, dtype=jnp.int32)

    def group_pieces(first_slot):
        live_mask = (first_slot + jnp.arange(group_size, dtype=jnp.int32) < live_count).astype(
            jnp.float32
        )
        return (coef_view, atom_table, rows_local, cols_local, live_mask)

    def forward_partial(values):
        table = values.reshape(fas_rows, BF)

        def forward_accumulate(turn, running):
            coef_blk, atom_blk, rows_blk, cols_blk, live_mask = group_pieces(turn * group_size)
            scaled = coef_blk.astype(jnp.float32) * table[cols_blk][:, None, :]
            image_blk = jnp.einsum(
                "kvj,kjd->kvd",
                scaled,
                atom_blk.astype(jnp.float32),
                precision=lax.Precision.HIGHEST,
                preferred_element_type=jnp.float32,
            )
            selector = (rows_blk[:, None] == vox_range[None, :]).astype(jnp.float32) * live_mask[
                :, None
            ]
            added = jnp.dot(
                selector.T,
                image_blk.reshape(group_size, row_width),
                precision=lax.Precision.HIGHEST,
                preferred_element_type=jnp.float32,
            )
            return running + added

        start = jnp.zeros((vox_rows, row_width), jnp.float32)
        return lax.fori_loop(0, group_turns, forward_accumulate, start)

    def backward_partial(rows_view):

        def backward_accumulate(turn, running):
            coef_blk, atom_blk, rows_blk, cols_blk, live_mask = group_pieces(turn * group_size)
            gathered = rows_view[rows_blk]
            inner = jnp.einsum(
                "kvj,kvd->kjd",
                coef_blk.astype(jnp.float32),
                gathered,
                precision=lax.Precision.HIGHEST,
                preferred_element_type=jnp.float32,
            )
            contrib = jnp.sum(atom_blk.astype(jnp.float32) * inner, axis=-1)
            selector = (cols_blk[:, None] == fas_range[None, :]).astype(jnp.float32) * live_mask[
                :, None
            ]
            added = jnp.dot(
                selector.T,
                contrib,
                precision=lax.Precision.HIGHEST,
                preferred_element_type=jnp.float32,
            )
            return running + added

        start = jnp.zeros((fas_rows, BF), jnp.float32)
        running = lax.fori_loop(0, group_turns, backward_accumulate, start)
        return running.reshape(-1)

    def collect(partial_value):
        return lax.psum_scatter(partial_value, "fas", scatter_dimension=1, tiled=True)

    weights = initial_weights
    residual = collect(forward_partial(weights)) - signal
    for sweep in range(ITERS):
        whole_rows = lax.all_gather(residual, "fas", axis=1, tiled=True)
        gradient = lax.psum(backward_partial(whole_rows.reshape(vox_rows, BV, DIRS)), "vox")
        projected = jnp.where((weights > 0) | (gradient < 0), gradient, 0.0)
        image_pred = collect(forward_partial(projected))
        image_local = jnp.sum(image_pred * image_pred)
        grad_sq = lax.psum(jnp.sum(projected * projected), "fas")
        image_sq = lax.psum(image_local, ("vox", "fas"))
        step_size = grad_sq / (image_sq + 1e-06)
        weights = jnp.maximum(weights - step_size * projected, 0.0)
        residual = collect(forward_partial(weights)) - signal
    return (weights, residual)


def solution(mesh):
    placed = (
        P("vox", "fas"),
        P("fas"),
        P(("vox", "fas"), None),
        P(("vox", "fas")),
        P(("vox", "fas")),
        P(("vox", "fas"), None),
        P(("vox", "fas")),
        P(),
    )
    return jax.shard_map(
        local, mesh=mesh, in_specs=placed, out_specs=(P("fas"), P("vox", "fas")), check_vma=False
    )
```

profile of v0, /device:TPU:0, one launch (start us, length us, event | category | flops | bytes accessed | tf_op | source)
XLA Modules:
  0.0 1822.5 jit_solution(13970018680334307103)
XLA Ops:
  18.6 57.4 %gather_fusion = bf16[16384,96]{1,0:T(8,128)(2,1)} fusion(bf16[360,96]{1,0:T(8,128)(2,1)S(1)} %copy.28, s32[16384]{0:T(1024)S(1)} %broadcast_clamp_fusion), kind=kCustom, calls=%fused_computation | custom fusion | bytes 6356992 | tf_op jit(solution)/shard_map/gather | solution.py:30
  76.7 27.9 %while.208 = (s32[]{:T(128)}, f32[16,6144]{1,0:T(8,128)S(1)}, s32[]{:T(128)}, s32[256]{0:T(256)S(1)}, s32[]{:T(128)}, /*index=5*/bf16[256,64,64]{2,1,0:T(8,128)(...) while((s32[]{:T(128)}, f32[16,6144]{1,0:T(8,128)S(1)}, ...), condition=%wide.region_1.2_spmd.clone, body=%wide.region_0.1_spmd.clone.sunk | while | flops 1512153856 | bytes 31263864 | solution.py:68
  105.5 64.2 %reduce-scatter.12.cloned.1.call-done = f32[16,768]{1,0:T(8,128)} async-done(((f32[16,6144]{1,0:T(8,128)}), f32[16,768]{1,0:T(8,128)}) %reduce-scatter.12.cloned.1.call-update) | async-done | bytes 49168 | tf_op jit(solution)/shard_map/reduce_scatter | solution.py:99
  170.5 31.4 %all_gather.15 = f32[16,6144]{1,0:T(8,128)S(1)} all-gather(f32[16,768]{1,0:T(8,128)S(1)} %sub.58), channel_id=1, replica_groups=mesh['vox'=4,'fas'=8] {'fas'}, dimensions={1}, use_global_device_ids=true | all-gather | bytes 442368 | tf_op jit(solution)/shard_map/all_gather | solution.py:104
  206.4 13.4 fusion.156
  222.1 30.6 %all-reduce.6.cloned.1.call-done = f32[32768]{0:T(1024)} async-done(((f32[32768]{0:T(1024)}), f32[32768]{0:T(1024)}) %all-reduce.6.cloned.1.call-update) | async-done | bytes 131088 | tf_op jit(solution)/shard_map/psum | solution.py:105
  255.0 28.3 %while.210 = (s32[]{:T(128)}, f32[16,6144]{1,0:T(8,128)S(1)}, s32[]{:T(128)}, s32[256]{0:T(256)S(1)}, s32[]{:T(128)}, /*index=5*/bf16[256,64,64]{2,1,0:T(8,128)(...) while((s32[]{:T(128)}, f32[16,6144]{1,0:T(8,128)S(1)}, ...), condition=%wide.region_10.11_spmd.clone, body=%wide.region_9.10_spmd.clone.sunk | while | flops 1512153856 | bytes 31263864 | solution.py:68
  284.2 61.4 %reduce-scatter.14.cloned.1.call-done = f32[16,768]{1,0:T(8,128)} async-done(((f32[16,6144]{1,0:T(8,128)}), f32[16,768]{1,0:T(8,128)}) %reduce-scatter.14.cloned.1.call-update) | async-done | bytes 49168 | tf_op jit(solution)/shard_map/reduce_scatter | solution.py:99
  347.1 20.1 %psum.106 = f32[]{:T(128)} all-reduce(f32[]{:T(128)} %get-tuple-element.2460), channel_id=1, replica_groups=mesh['vox'=4,'fas'=8] {'fas'}, use_global_device_ids=true, to_apply=%region_8.9 | all-reduce | flops 1 | bytes 8 | tf_op jit(solution)/shard_map/psum | solution.py:109
  367.2 37.1 %psum.107 = f32[]{:T(128)} all-reduce(f32[]{:T(128)} %multiply_reduce_fusion.9), channel_id=1, replica_groups=mesh['vox'=4,'fas'=8] {'vox','fas'}, use_global_device_ids=true, to_apply=%region_13.14 | all-reduce | flops 1 | bytes 8 | tf_op jit(solution)/shard_map/psum | solution.py:110
  406.5 28.1 %while.211 = (s32[]{:T(128)}, f32[16,6144]{1,0:T(8,128)S(1)}, s32[]{:T(128)}, s32[256]{0:T(256)S(1)}, s32[]{:T(128)}, /*index=5*/bf16[256,64,64]{2,1,0:T(8,128)(...) while((s32[]{:T(128)}, f32[16,6144]{1,0:T(8,128)S(1)}, ...), condition=%wide.region_15.16_spmd.clone, body=%wide.region_14.15_spmd.clone.sunk | while | flops 1512153856 | bytes 31263864 | solution.py:68
  435.4 63.1 %reduce-scatter.16.cloned.1.call-done = f32[16,768]{1,0:T(8,128)} async-done(((f32[16,6144]{1,0:T(8,128)}), f32[16,768]{1,0:T(8,128)}) %reduce-scatter.16.cloned.1.call-update) | async-done | bytes 49168 | tf_op jit(solution)/shard_map/reduce_scatter | solution.py:99
  499.3 31.3 %all_gather.16 = f32[16,6144]{1,0:T(8,128)S(1)} all-gather(f32[16,768]{1,0:T(8,128)S(1)} %sub.60), channel_id=1, replica_groups=mesh['vox'=4,'fas'=8] {'fas'}, dimensions={1}, use_global_device_ids=true | all-gather | bytes 442368 | tf_op jit(solution)/shard_map/all_gather | solution.py:104
  535.2 13.4 fusion.157
  550.9 30.7 %all-reduce.8.cloned.1.call-done = f32[32768]{0:T(1024)} async-done(((f32[32768]{0:T(1024)}), f32[32768]{0:T(1024)}) %all-reduce.8.cloned.1.call-update) | async-done | bytes 131088 | tf_op jit(solution)/shard_map/psum | solution.py:105
  584.0 28.2 %while.213 = (s32[]{:T(128)}, f32[16,6144]{1,0:T(8,128)S(1)}, s32[]{:T(128)}, s32[256]{0:T(256)S(1)}, s32[]{:T(128)}, /*index=5*/bf16[256,64,64]{2,1,0:T(8,128)(...) while((s32[]{:T(128)}, f32[16,6144]{1,0:T(8,128)S(1)}, ...), condition=%wide.region_24.25_spmd.clone, body=%wide.region_23.24_spmd.clone.sunk | while | flops 1512153856 | bytes 31263864 | solution.py:68
  613.0 61.4 %reduce-scatter.18.cloned.1.call-done = f32[16,768]{1,0:T(8,128)} async-done(((f32[16,6144]{1,0:T(8,128)}), f32[16,768]{1,0:T(8,128)}) %reduce-scatter.18.cloned.1.call-update) | async-done | bytes 49168 | tf_op jit(solution)/shard_map/reduce_scatter | solution.py:99
  675.9 20.1 %psum.109 = f32[]{:T(128)} all-reduce(f32[]{:T(128)} %get-tuple-element.2458), channel_id=1, replica_groups=mesh['vox'=4,'fas'=8] {'fas'}, use_global_device_ids=true, to_apply=%region_22.23 | all-reduce | flops 1 | bytes 8 | tf_op jit(solution)/shard_map/psum | solution.py:109
  696.0 37.1 %psum.110 = f32[]{:T(128)} all-reduce(f32[]{:T(128)} %multiply_reduce_fusion.8), channel_id=1, replica_groups=mesh['vox'=4,'fas'=8] {'vox','fas'}, use_global_device_ids=true, to_apply=%region_27.28 | all-reduce | flops 1 | bytes 8 | tf_op jit(solution)/shard_map/psum | solution.py:110
  735.3 28.4 %while.214 = (s32[]{:T(128)}, f32[16,6144]{1,0:T(8,128)S(1)}, s32[]{:T(128)}, s32[256]{0:T(256)S(1)}, s32[]{:T(128)}, /*index=5*/bf16[256,64,64]{2,1,0:T(8,128)(...) while((s32[]{:T(128)}, f32[16,6144]{1,0:T(8,128)S(1)}, ...), condition=%wide.region_29.30_spmd.clone, body=%wide.region_28.29_spmd.clone.sunk | while | flops 1512153856 | bytes 31263864 | solution.py:68
  764.5 63.1 %reduce-scatter.20.cloned.1.call-done = f32[16,768]{1,0:T(8,128)} async-done(((f32[16,6144]{1,0:T(8,128)}), f32[16,768]{1,0:T(8,128)}) %reduce-scatter.20.cloned.1.call-update) | async-done | bytes 49168 | tf_op jit(solution)/shard_map/reduce_scatter | solution.py:99
  828.4 31.3 %all_gather.17 = f32[16,6144]{1,0:T(8,128)S(1)} all-gather(f32[16,768]{1,0:T(8,128)S(1)} %sub.62), channel_id=1, replica_groups=mesh['vox'=4,'fas'=8] {'fas'}, dimensions={1}, use_global_device_ids=true | all-gather | bytes 442368 | tf_op jit(solution)/shard_map/all_gather | solution.py:104
  864.3 13.4 fusion.158
  880.0 30.6 %all-reduce.10.cloned.1.call-done = f32[32768]{0:T(1024)} async-done(((f32[32768]{0:T(1024)}), f32[32768]{0:T(1024)}) %all-reduce.10.cloned.1.call-update) | async-done | bytes 131088 | tf_op jit(solution)/shard_map/psum | solution.py:105
  913.0 28.1 %while.216 = (s32[]{:T(128)}, f32[16,6144]{1,0:T(8,128)S(1)}, s32[]{:T(128)}, s32[256]{0:T(256)S(1)}, s32[]{:T(128)}, /*index=5*/bf16[256,64,64]{2,1,0:T(8,128)(...) while((s32[]{:T(128)}, f32[16,6144]{1,0:T(8,128)S(1)}, ...), condition=%wide.region_38.39_spmd.clone, body=%wide.region_37.38_spmd.clone.sunk | while | flops 1512153856 | bytes 31263864 | solution.py:68
  941.9 61.4 %reduce-scatter.22.cloned.1.call-done = f32[16,768]{1,0:T(8,128)} async-done(((f32[16,6144]{1,0:T(8,128)}), f32[16,768]{1,0:T(8,128)}) %reduce-scatter.22.cloned.1.call-update) | async-done | bytes 49168 | tf_op jit(solution)/shard_map/reduce_scatter | solution.py:99
  1004.9 20.1 %psum.112 = f32[]{:T(128)} all-reduce(f32[]{:T(128)} %get-tuple-element.2456), channel_id=1, replica_groups=mesh['vox'=4,'fas'=8] {'fas'}, use_global_device_ids=true, to_apply=%region_36.37 | all-reduce | flops 1 | bytes 8 | tf_op jit(solution)/shard_map/psum | solution.py:109
  1024.9 37.1 %psum.113 = f32[]{:T(128)} all-reduce(f32[]{:T(128)} %multiply_reduce_fusion.7), channel_id=1, replica_groups=mesh['vox'=4,'fas'=8] {'vox','fas'}, use_global_device_ids=true, to_apply=%region_41.42 | all-reduce | flops 1 | bytes 8 | tf_op jit(solution)/shard_map/psum | solution.py:110
  1064.3 28.3 %while.217 = (s32[]{:T(128)}, f32[16,6144]{1,0:T(8,128)S(1)}, s32[]{:T(128)}, s32[256]{0:T(256)S(1)}, s32[]{:T(128)}, /*index=5*/bf16[256,64,64]{2,1,0:T(8,128)(...) while((s32[]{:T(128)}, f32[16,6144]{1,0:T(8,128)S(1)}, ...), condition=%wide.region_43.44_spmd.clone, body=%wide.region_42.43_spmd.clone.sunk | while | flops 1512153856 | bytes 31263864 | solution.py:68
  1093.4 63.1 %reduce-scatter.24.cloned.1.call-done = f32[16,768]{1,0:T(8,128)} async-done(((f32[16,6144]{1,0:T(8,128)}), f32[16,768]{1,0:T(8,128)}) %reduce-scatter.24.cloned.1.call-update) | async-done | bytes 49168 | tf_op jit(solution)/shard_map/reduce_scatter | solution.py:99
  1157.3 31.3 %all_gather.18 = f32[16,6144]{1,0:T(8,128)S(1)} all-gather(f32[16,768]{1,0:T(8,128)S(1)} %sub.64), channel_id=1, replica_groups=mesh['vox'=4,'fas'=8] {'fas'}, dimensions={1}, use_global_device_ids=true | all-gather | bytes 442368 | tf_op jit(solution)/shard_map/all_gather | solution.py:104
  1193.2 13.4 fusion.159
  1208.9 30.6 %all-reduce.12.cloned.1.call-done = f32[32768]{0:T(1024)} async-done(((f32[32768]{0:T(1024)}), f32[32768]{0:T(1024)}) %all-reduce.12.cloned.1.call-update) | async-done | bytes 131088 | tf_op jit(solution)/shard_map/psum | solution.py:105
  1241.9 28.1 %while.219 = (s32[]{:T(128)}, f32[16,6144]{1,0:T(8,128)S(1)}, s32[]{:T(128)}, s32[256]{0:T(256)S(1)}, s32[]{:T(128)}, /*index=5*/bf16[256,64,64]{2,1,0:T(8,128)(...) while((s32[]{:T(128)}, f32[16,6144]{1,0:T(8,128)S(1)}, ...), condition=%wide.region_52.53_spmd.clone, body=%wide.region_51.52_spmd.clone.sunk | while | flops 1512153856 | bytes 31263864 | solution.py:68
  1270.9 61.4 %reduce-scatter.26.cloned.1.call-done = f32[16,768]{1,0:T(8,128)} async-done(((f32[16,6144]{1,0:T(8,128)}), f32[16,768]{1,0:T(8,128)}) %reduce-scatter.26.cloned.1.call-update) | async-done | bytes 49168 | tf_op jit(solution)/shard_map/reduce_scatter | solution.py:99
  1333.8 20.1 %psum.115 = f32[]{:T(128)} all-reduce(f32[]{:T(128)} %get-tuple-element.2454), channel_id=1, replica_groups=mesh['vox'=4,'fas'=8] {'fas'}, use_global_device_ids=true, to_apply=%region_50.51 | all-reduce | flops 1 | bytes 8 | tf_op jit(solution)/shard_map/psum | solution.py:109
  1353.9 37.1 %psum.116 = f32[]{:T(128)} all-reduce(f32[]{:T(128)} %multiply_reduce_fusion.6), channel_id=1, replica_groups=mesh['vox'=4,'fas'=8] {'vox','fas'}, use_global_device_ids=true, to_apply=%region_55.56 | all-reduce | flops 1 | bytes 8 | tf_op jit(solution)/shard_map/psum | solution.py:110
  1393.2 28.3 %while.220 = (s32[]{:T(128)}, f32[16,6144]{1,0:T(8,128)S(1)}, s32[]{:T(128)}, s32[256]{0:T(256)S(1)}, s32[]{:T(128)}, /*index=5*/bf16[256,64,64]{2,1,0:T(8,128)(...) while((s32[]{:T(128)}, f32[16,6144]{1,0:T(8,128)S(1)}, ...), condition=%wide.region_57.58_spmd.clone, body=%wide.region_56.57_spmd.clone.sunk | while | flops 1512153856 | bytes 31263864 | solution.py:68
  1422.4 63.1 %reduce-scatter.28.cloned.1.call-done = f32[16,768]{1,0:T(8,128)} async-done(((f32[16,6144]{1,0:T(8,128)}), f32[16,768]{1,0:T(8,128)}) %reduce-scatter.28.cloned.1.call-update) | async-done | bytes 49168 | tf_op jit(solution)/shard_map/reduce_scatter | solution.py:99
  1486.3 31.3 %all_gather.19 = f32[16,6144]{1,0:T(8,128)S(1)} all-gather(f32[16,768]{1,0:T(8,128)S(1)} %sub.66), channel_id=1, replica_groups=mesh['vox'=4,'fas'=8] {'fas'}, dimensions={1}, use_global_device_ids=true | all-gather | bytes 442368 | tf_op jit(solution)/shard_map/all_gather | solution.py:104
  1522.2 13.4 fusion.160
  1537.8 30.5 %all-reduce.14.cloned.1.call-done = f32[32768]{0:T(1024)} async-done(((f32[32768]{0:T(1024)}), f32[32768]{0:T(1024)}) %all-reduce.14.cloned.1.call-update) | async-done | bytes 131088 | tf_op jit(solution)/shard_map/psum | solution.py:105
  1570.8 28.1 %while.222 = (s32[]{:T(128)}, f32[16,6144]{1,0:T(8,128)S(1)}, s32[]{:T(128)}, s32[256]{0:T(256)S(1)}, s32[]{:T(128)}, /*index=5*/bf16[256,64,64]{2,1,0:T(8,128)(...) while((s32[]{:T(128)}, f32[16,6144]{1,0:T(8,128)S(1)}, ...), condition=%wide.region_66.67_spmd.clone, body=%wide.region_65.66_spmd.clone.sunk | while | flops 1512153856 | bytes 31263864 | solution.py:68
  1599.7 61.5 %reduce-scatter.30.cloned.1.call-done = f32[16,768]{1,0:T(8,128)} async-done(((f32[16,6144]{1,0:T(8,128)}), f32[16,768]{1,0:T(8,128)}) %reduce-scatter.30.cloned.1.call-update) | async-done | bytes 49168 | tf_op jit(solution)/shard_map/reduce_scatter | solution.py:99
  1662.7 20.0 %psum.118 = f32[]{:T(128)} all-reduce(f32[]{:T(128)} %get-tuple-element.2452), channel_id=1, replica_groups=mesh['vox'=4,'fas'=8] {'fas'}, use_global_device_ids=true, to_apply=%region_64.65 | all-reduce | flops 1 | bytes 8 | tf_op jit(solution)/shard_map/psum | solution.py:109
  1682.7 37.1 %psum.119 = f32[]{:T(128)} all-reduce(f32[]{:T(128)} %multiply_reduce_fusion.5), channel_id=1, replica_groups=mesh['vox'=4,'fas'=8] {'vox','fas'}, use_global_device_ids=true, to_apply=%region_69.70 | all-reduce | flops 1 | bytes 8 | tf_op jit(solution)/shard_map/psum | solution.py:110
  1722.1 28.2 %while.223 = (s32[]{:T(128)}, f32[16,6144]{1,0:T(8,128)S(1)}, s32[]{:T(128)}, s32[256]{0:T(256)S(1)}, s32[]{:T(128)}, /*index=5*/bf16[256,64,64]{2,1,0:T(8,128)(...) while((s32[]{:T(128)}, f32[16,6144]{1,0:T(8,128)S(1)}, ...), condition=%wide.region_71.72_spmd.clone, body=%wide.region_70.71_spmd.clone.sunk | while | flops 1512153856 | bytes 31263864 | solution.py:68
  1751.0 63.1 %reduce-scatter.32.cloned.1.call-done = f32[16,768]{1,0:T(8,128)} async-done(((f32[16,6144]{1,0:T(8,128)}), f32[16,768]{1,0:T(8,128)}) %reduce-scatter.32.cloned.1.call-update) | async-done | bytes 49168 | tf_op jit(solution)/shard_map/reduce_scatter | solution.py:99
  (217 shorter events, 395.9 us)
Async XLA Ops:
  7.2 10.8 copy-start.15
  7.2 11.1 copy-start.14
  7.2 11.2 copy-start.16
  7.2 11.2 copy-start.11
  7.2 162.4 %reduce-scatter.12.cloned.1.call-start = ((), (), s32[]{:S(2)}) async-start(), calls=%async_computation.11 | async-start | bytes 442368 | tf_op jit(solution)/shard_map/reduce_scatter | solution.py:99
  18.5 58.1 %copy-start.17 = (s32[256]{0:T(256)S(1)}, s32[256]{0:T(256)}, u32[]{:S(2)}) copy-start(s32[256]{0:T(256)} %param.43) | copy-start | bytes 3076
  76.7 92.9 %copy-start.12 = (f32[16,768]{1,0:T(8,128)S(1)}, f32[16,768]{1,0:T(8,128)}, u32[]{:S(2)}) copy-start(f32[16,768]{1,0:T(8,128)} %param.40) | copy-start | bytes 147460
  104.6 0.7 copy-start.1
  105.4 147.2 %all-reduce.6.cloned.1.call-start = ((), (), s32[]{:S(2)}) async-start(), calls=%async_computation.12 | async-start | bytes 262144 | tf_op jit(solution)/shard_map/psum | solution.py:105
  222.0 123.6 %reduce-scatter.14.cloned.1.call-start = ((), (), s32[]{:S(2)}) async-start(), calls=%async_computation.13 | async-start | bytes 442368 | tf_op jit(solution)/shard_map/reduce_scatter | solution.py:99
  283.4 0.7 copy-start.2
  284.1 214.4 %reduce-scatter.16.cloned.1.call-start = ((), (), s32[]{:S(2)}) async-start(), calls=%async_computation.14 | async-start | bytes 442368 | tf_op jit(solution)/shard_map/reduce_scatter | solution.py:99
  434.6 0.7 copy-start.3
  435.4 146.2 %all-reduce.8.cloned.1.call-start = ((), (), s32[]{:S(2)}) async-start(), calls=%async_computation.15 | async-start | bytes 262144 | tf_op jit(solution)/shard_map/psum | solution.py:105
  550.8 123.6 %reduce-scatter.18.cloned.1.call-start = ((), (), s32[]{:S(2)}) async-start(), calls=%async_computation.16 | async-start | bytes 442368 | tf_op jit(solution)/shard_map/reduce_scatter | solution.py:99
  612.1 0.7 copy-start.4
  612.9 214.7 %reduce-scatter.20.cloned.1.call-start = ((), (), s32[]{:S(2)}) async-start(), calls=%async_computation.17 | async-start | bytes 442368 | tf_op jit(solution)/shard_map/reduce_scatter | solution.py:99
  763.7 0.7 copy-start.5
  764.5 146.1 %all-reduce.10.cloned.1.call-start = ((), (), s32[]{:S(2)}) async-start(), calls=%async_computation.18 | async-start | bytes 262144 | tf_op jit(solution)/shard_map/psum | solution.py:105
  879.9 123.5 %reduce-scatter.22.cloned.1.call-start = ((), (), s32[]{:S(2)}) async-start(), calls=%async_computation.19 | async-start | bytes 442368 | tf_op jit(solution)/shard_map/reduce_scatter | solution.py:99
  941.1 0.7 copy-start.6
  941.9 214.6 %reduce-scatter.24.cloned.1.call-start = ((), (), s32[]{:S(2)}) async-start(), calls=%async_computation.20 | async-start | bytes 442368 | tf_op jit(solution)/shard_map/reduce_scatter | solution.py:99
  1092.6 0.7 copy-start.7
  1093.4 146.1 %all-reduce.12.cloned.1.call-start = ((), (), s32[]{:S(2)}) async-start(), calls=%async_computation.21 | async-start | bytes 262144 | tf_op jit(solution)/shard_map/psum | solution.py:105
  1208.8 123.5 %reduce-scatter.26.cloned.1.call-start = ((), (), s32[]{:S(2)}) async-start(), calls=%async_computation.22 | async-start | bytes 442368 | tf_op jit(solution)/shard_map/reduce_scatter | solution.py:99
  1270.0 0.7 copy-start.8
  1270.8 214.7 %reduce-scatter.28.cloned.1.call-start = ((), (), s32[]{:S(2)}) async-start(), calls=%async_computation.23 | async-start | bytes 442368 | tf_op jit(solution)/shard_map/reduce_scatter | solution.py:99
  1421.5 0.7 copy-start.9
  1422.3 146.0 %all-reduce.14.cloned.1.call-start = ((), (), s32[]{:S(2)}) async-start(), calls=%async_computation.24 | async-start | bytes 262144 | tf_op jit(solution)/shard_map/psum | solution.py:105
  1537.8 123.4 %reduce-scatter.30.cloned.1.call-start = ((), (), s32[]{:S(2)}) async-start(), calls=%async_computation.25 | async-start | bytes 442368 | tf_op jit(solution)/shard_map/reduce_scatter | solution.py:99
  1598.9 0.7 copy-start.10
  1599.7 214.5 %reduce-scatter.32.cloned.1.call-start = ((), (), s32[]{:S(2)}) async-start(), calls=%async_computation.26 | async-start | bytes 442368 | tf_op jit(solution)/shard_map/reduce_scatter | solution.py:99
  1721.2 0.9 copy-start.13
  1750.3 0.7 copy-start
Sparse Core Ops, SparseCore 0:
  105.5 64.0 reduce-scatter.11
  222.1 30.4 all-reduce.5
  284.2 61.3 reduce-scatter.13
  435.5 62.9 reduce-scatter.15
  550.9 30.5 all-reduce.7
  613.0 61.3 reduce-scatter.17
  764.6 62.9 reduce-scatter.19
  880.0 30.4 all-reduce.9
  942.0 61.3 reduce-scatter.21
  1093.5 62.9 reduce-scatter.23
  1208.9 30.5 all-reduce.11
  1270.9 61.3 reduce-scatter.25
  1422.4 62.9 reduce-scatter.27
  1537.9 30.4 all-reduce.13
  1599.8 61.3 reduce-scatter.29
  1751.2 62.9 reduce-scatter.31
where the time goes:
time: 1830 us; the launch traced here: 1820 us
  waiting for transfers between devices  840 us (46%)
  blocking collectives  442 us (24%)
  matrix products  275 us (15%)
  local copies, waits for them, and re-layouts  207 us (11%)
  other arithmetic  31.2 us (2%)
  between operations  22.6 us (1%)
    reduce_scatter x11, waiting for transfers between devices, collect(): lax.psum_scatter(partial_value, 'fas', scatter_dimension=1, tiled=True)  687 us
    psum x5, blocking collectives, local(): image_sq = lax.psum(image_local, ('vox', 'fas'))  185 us
    all_gather x5, blocking collectives, local(): whole_rows = lax.all_gather(residual, 'fas', axis=1, tiled=True)  157 us
    psum x5, waiting for transfers between devices, local(): lax.psum(backward_partial(whole_rows.reshape(vox_rows, BV, DIRS)), 'vox')  153 us
    dot_general x11, matrix products, forward_accumulate(): jnp.einsum('kvj,kjd->kvd', scaled, atom_blk.astype(jnp.float32), precisio...  124 us
    psum x5, blocking collectives, local(): grad_sq = lax.psum(jnp.sum(projected * projected), 'fas')  100 us
    dot_general x11, local copies, waits for them, and re-layouts, forward_accumulate(): jnp.einsum('kvj,kjd->kvd', scaled, atom_blk.astype(jnp.float32), precisio...  94.4 us
    dot_general x11, matrix products, forward_accumulate(): jnp.dot(selector.T, image_blk.reshape(group_size, row_width), precision=l...  81.8 us
  transfers between devices with their start and end apart: 16, of which 16 were waited for; matrix products, arithmetic and copies ran while one was open for 0% of the time, Pallas kernels for 0%

commit v1 on v0

v1 whole, which is shorter than its diff:
```python
import functools

import jax
import jax.numpy as jnp
from jax import lax
from jax.experimental import pallas as pl
from jax.experimental.pallas import tpu as pltpu
from jax.sharding import PartitionSpec as P

BV = 64
BF = 64
DIRS = 96
ITERS = 5
LANES = 128
GROUP = 4
UNROLL = 4
PACK = BV * DIRS // LANES
HALF = BV // 2
QUART = BV // 4
VMEM_LIMIT = 48 * 1024 * 1024


def group_cap(slots, rows):
    groups = slots // GROUP + rows
    return -(-groups // UNROLL) * UNROLL


def lane_ids(rows):
    return lax.broadcasted_iota(jnp.int32, (rows, LANES), 1)


def setup_kernel(
    vox_rows,
    fas_rows,
    cap,
    rows_ref,
    cols_ref,
    count_ref,
    coef_ref,
    atom_ref,
    dict_ref,
    cp_ref,
    at_ref,
    a_ref,
    meta_ref,
    place_ref,
    slot_ref,
):
    slots = coef_ref.shape[0]
    live = count_ref[0]

    def clear_row(r, carry):
        place_ref[r] = 0
        return carry

    lax.fori_loop(0, vox_rows, clear_row, 0)

    def count_row(k, carry):
        r = lax.rem(rows_ref[k], vox_rows)
        place_ref[r] = place_ref[r] + 1
        return carry

    lax.fori_loop(0, live, count_row, 0)

    def clear_slot(p, carry):
        slot_ref[p] = -1
        meta_ref[p] = 0
        return carry

    lax.fori_loop(0, cap * GROUP, clear_slot, 0)

    def clear_group(q, carry):
        meta_ref[cap * GROUP + q] = 0
        return carry

    lax.fori_loop(0, cap, clear_group, 0)

    def place_row(r, start):
        groups = (place_ref[r] + GROUP - 1) // GROUP
        place_ref[r] = start * GROUP

        def name_group(q, carry):
            meta_ref[cap * GROUP + q] = r
            return carry

        lax.fori_loop(start, start + groups, name_group, 0)
        return start + groups

    total = lax.fori_loop(0, vox_rows, place_row, 0)
    turns = (total + UNROLL - 1) // UNROLL
    meta_ref[cap * (GROUP + 1)] = turns

    def place_slot(k, carry):
        r = lax.rem(rows_ref[k], vox_rows)
        p = place_ref[r]
        place_ref[r] = p + 1
        slot_ref[p] = k
        meta_ref[p] = lax.rem(cols_ref[k], fas_rows)
        return carry

    lax.fori_loop(0, live, place_slot, 0)

    atoms_pad = dict_ref.shape[1]
    left32 = lane_ids(HALF) < BF
    left1 = lane_ids(1) < BF
    atom_ids = lax.broadcasted_iota(jnp.int32, (atoms_pad, LANES), 0)

    def build(q, carry):
        tops, bottoms, marks = [], [], []
        for pair in range(GROUP // 2):
            s0 = slot_ref[q * GROUP + 2 * pair]
            s1 = slot_ref[q * GROUP + 2 * pair + 1]
            k0 = jnp.maximum(s0, 0)
            k1 = jnp.maximum(s1, 0)
            m0 = (s0 >= 0).astype(jnp.float32)
            m1 = (s1 >= 0).astype(jnp.float32)
            c0 = coef_ref[k0].astype(jnp.float32) * m0
            c1 = coef_ref[k1].astype(jnp.float32) * m1
            tops.append(jnp.where(left32, c0, pltpu.roll(c1, BF, 1)))
            bottoms.append(jnp.where(left32, pltpu.roll(c0, BF, 1), c1))
            ids = jnp.where(left1, atom_ref[pl.ds(k0, 1), :], atom_ref[pl.ds(k1, 1), :])
            marks.append((atom_ids == ids).astype(jnp.float32).astype(jnp.bfloat16))
        top = jnp.concatenate(tops, axis=1)
        bottom = jnp.concatenate(bottoms, axis=1)
        cp_ref[q] = jnp.concatenate([top, bottom], axis=0).astype(jnp.bfloat16)
        marked = jnp.concatenate(marks, axis=1)
        table = jnp.dot(dict_ref[...], marked, preferred_element_type=jnp.float32)
        at_ref[q] = table.astype(jnp.bfloat16)
        a_ref[q] = table.T.astype(jnp.bfloat16)
        return carry

    lax.fori_loop(0, turns * UNROLL, build, 0)


def spread_table(values, table_ref):
    rows = values.shape[0]
    left = lane_ids(rows) < BF
    turned = pltpu.roll(values, BF, 1)
    table_ref[pl.ds(0, rows, stride=2), :] = jnp.where(left, values, turned)
    table_ref[pl.ds(1, rows, stride=2), :] = jnp.where(left, turned, values)


def run_forward(cap, meta_ref, cp_ref, a_ref, table_ref, acc_ref):
    left = lane_ids(1) < BF

    def turn(t, carry):
        outs = []
        for n in range(UNROLL):
            q = t * UNROLL + n
            u = []
            for pair in range(GROUP // 2):
                p = q * GROUP + 2 * pair
                u0 = table_ref[pl.ds(meta_ref[p], 1), :]
                u1 = table_ref[pl.ds(meta_ref[p + 1], 1), :]
                u.append(jnp.where(left, u0, u1))
            scaled = cp_ref[q].astype(jnp.float32) * jnp.concatenate(u, axis=1)
            high = scaled.astype(jnp.bfloat16)
            low = (scaled - high.astype(jnp.float32)).astype(jnp.bfloat16)
            both = jnp.concatenate([high, low], axis=0)
            out = jnp.dot(both, a_ref[q], preferred_element_type=jnp.float32)
            outs.append(out[:BV] + out[BV:])
        for n in range(UNROLL):
            r = meta_ref[cap * GROUP + t * UNROLL + n]
            acc_ref[r] = acc_ref[r] + outs[n]
        return carry

    lax.fori_loop(0, meta_ref[cap * (GROUP + 1)], turn, 0)


def pack_rows(acc_ref, out_ref):
    lane = lane_ids(QUART)
    for r in range(acc_ref.shape[0]):
        last = acc_ref[r, 3 * QUART :, :]
        for i in range(3):
            tail = pltpu.roll(last, DIRS - 32 * i, 1)
            out_ref[pl.ds(r * PACK + i * QUART, QUART), :] = jnp.where(
                lane < DIRS, acc_ref[r, i * QUART : (i + 1) * QUART, :], tail
            )


def first_kernel(cap, meta_ref, w_ref, sig_ref, cp_ref, a_ref, out_ref, table_ref, acc_ref):
    spread_table(w_ref[...], table_ref)
    acc_ref[...] = sig_ref[...]
    run_forward(cap, meta_ref, cp_ref, a_ref, table_ref, acc_ref)
    pack_rows(acc_ref, out_ref)


def image_kernel(cap, meta_ref, g_ref, w_ref, cp_ref, a_ref, out_ref, p_ref, sq_ref, table_ref, acc_ref):
    gradient = g_ref[...]
    projected = jnp.where((w_ref[...] > 0) | (gradient < 0), gradient, 0.0)
    p_ref[...] = projected
    sq_ref[...] = jnp.sum((projected * projected).reshape(-1, 8, LANES), axis=0)
    spread_table(projected, table_ref)
    acc_ref[...] = jnp.zeros_like(acc_ref)
    run_forward(cap, meta_ref, cp_ref, a_ref, table_ref, acc_ref)
    pack_rows(acc_ref, out_ref)


def update_kernel(
    cap,
    vox_total,
    last,
    meta_ref,
    sums_ref,
    p_ref,
    w_ref,
    sig_ref,
    cp_ref,
    a_ref,
    out_ref,
    new_ref,
    table_ref,
    acc_ref,
):
    sums = jnp.sum(sums_ref[...], axis=0)
    upper = lax.broadcasted_iota(jnp.int32, (8, LANES), 0) < 4
    image_sq = jnp.sum(jnp.where(upper, sums, 0.0), keepdims=True)
    grad_sq = jnp.sum(jnp.where(upper, 0.0, sums), keepdims=True) * (1.0 / vox_total)
    step = grad_sq / (image_sq + 1e-6)
    updated = jnp.maximum(w_ref[...] - step * p_ref[...], 0.0)
    new_ref[...] = updated
    spread_table(updated, table_ref)
    acc_ref[...] = sig_ref[...]
    run_forward(cap, meta_ref, cp_ref, a_ref, table_ref, acc_ref)
    if last:
        out_ref[...] = acc_ref[...]
    else:
        pack_rows(acc_ref, out_ref)


def backward_kernel(cap, vox_rows, meta_ref, res_ref, cp_ref, at_ref, out_ref, split_ref, table_ref):
    lane = lane_ids(QUART)
    for r in range(vox_rows):
        packed = [res_ref[pl.ds(r * PACK + i * QUART, QUART), :] for i in range(3)]
        turned = [pltpu.roll(packed[i], 32 * (i + 1), 1) for i in range(3)]
        last = jnp.where(lane < 32, turned[0], jnp.where(lane < 64, turned[1], turned[2]))
        whole = jnp.concatenate(packed + [last], axis=0)
        whole = jnp.where(lane_ids(BV) < DIRS, whole, 0.0)
        high = whole.astype(jnp.bfloat16)
        low = (whole - high.astype(jnp.float32)).astype(jnp.bfloat16)
        split_ref[r] = jnp.concatenate([high, low], axis=0)
    table_ref[...] = jnp.zeros_like(table_ref)
    left = lane_ids(1) < BF

    def turn(t, carry):
        sums = []
        for n in range(UNROLL):
            q = t * UNROLL + n
            r = meta_ref[cap * GROUP + q]
            part = jnp.dot(split_ref[r], at_ref[q], preferred_element_type=jnp.float32)
            part = (part[:BV] + part[BV:]) * cp_ref[q].astype(jnp.float32)
            sums.append(jnp.sum(part, axis=0, keepdims=True))
        for n in range(UNROLL):
            for pair in range(GROUP // 2):
                p = (t * UNROLL + n) * GROUP + 2 * pair
                row = sums[n][:, pair * LANES : (pair + 1) * LANES]
                c0 = pl.ds(meta_ref[p], 1)
                table_ref[c0, :] = table_ref[c0, :] + jnp.where(left, row, 0.0)
                c1 = pl.ds(meta_ref[p + 1], 1)
                table_ref[c1, :] = table_ref[c1, :] + jnp.where(left, 0.0, row)
        return carry

    lax.fori_loop(0, meta_ref[cap * (GROUP + 1)], turn, 0)
    rows = out_ref.shape[0]
    even = table_ref[pl.ds(0, rows, stride=2), :]
    odd = table_ref[pl.ds(1, rows, stride=2), :]
    even = even + pltpu.roll(even, BF, 1)
    odd = odd + pltpu.roll(odd, BF, 1)
    out_ref[...] = jnp.where(lane_ids(rows) < BF, even, odd)


def call(kernel, outs, ins, scratch=()):
    spaces = {"v": pltpu.VMEM, "s": pltpu.SMEM}
    return pl.pallas_call(
        kernel,
        out_shape=tuple(jax.ShapeDtypeStruct(shape, dtype) for shape, dtype, _ in outs),
        in_specs=[pl.BlockSpec(memory_space=spaces[kind]) for kind in ins],
        out_specs=tuple(pl.BlockSpec(memory_space=spaces[kind]) for _, _, kind in outs),
        scratch_shapes=list(scratch),
        compiler_params=pltpu.CompilerParams(vmem_limit_bytes=VMEM_LIMIT),
    )


def local(
    n_vox,
    n_fas,
    signal,
    initial_weights,
    coefficients,
    block_rows,
    block_cols,
    block_atoms,
    block_count,
    dictionary,
):
    f32, bf16, i32 = jnp.float32, jnp.bfloat16, jnp.int32
    vox_rows = signal.shape[0]
    fas_rows = initial_weights.shape[0] // BF
    slots = coefficients.shape[0]
    cap = group_cap(slots, vox_rows)
    atoms = dictionary.shape[0]
    atoms_pad = -(-atoms // LANES) * LANES
    meta_size = -(-(cap * (GROUP + 1) + 1) // LANES) * LANES
    wide = GROUP * BF
    half_rows = fas_rows // 2

    coef_view = coefficients.reshape(slots, HALF, LANES)
    atom_view = jnp.concatenate([block_atoms, block_atoms], axis=1)
    dict_t = jnp.pad(dictionary.T, ((0, LANES - DIRS), (0, atoms_pad - atoms)))

    cp, at, a, meta = call(
        functools.partial(setup_kernel, vox_rows, fas_rows, cap),
        [
            ((cap, BV, wide), bf16, "v"),
            ((cap, LANES, wide), bf16, "v"),
            ((cap, wide, LANES), bf16, "v"),
            ((meta_size,), i32, "s"),
        ],
        "sssvvv",
        [pltpu.SMEM((vox_rows,), i32), pltpu.SMEM((cap * GROUP,), i32)],
    )(block_rows, block_cols, block_count, coef_view, atom_view, dict_t)

    own = signal.shape[1] // DIRS // 2
    fas_place = lax.axis_index("fas")
    negative = -signal.reshape(vox_rows, own, 2, DIRS).transpose(0, 2, 1, 3)
    negative = jnp.pad(negative, ((0, 0), (0, 0), (0, 0), (0, LANES - DIRS)))
    sig = lax.dynamic_update_slice(
        jnp.zeros((vox_rows, 2, HALF, LANES), f32), negative, (0, 0, fas_place * own, 0)
    ).reshape(vox_rows, BV, LANES)

    image_rows = vox_rows * PACK
    table = pltpu.VMEM((fas_rows, LANES), f32)
    acc = pltpu.VMEM((vox_rows, BV, LANES), f32)
    image_out = ((image_rows, LANES), f32, "v")
    flat_out = ((half_rows, LANES), f32, "v")

    def swap(x, axis):
        return lax.all_to_all(x, axis, 0, 0)

    def collect(partial):
        shares = swap(partial.reshape(n_fas, image_rows // n_fas, LANES), "fas")
        return jnp.sum(shares, axis=0)

    weights = initial_weights.reshape(half_rows, LANES)
    (partial,) = call(
        functools.partial(first_kernel, cap), [image_out], "svvvv", [table, acc]
    )(meta, weights, sig, cp, a)
    for sweep in range(ITERS):
        last = sweep == ITERS - 1
        residual = collect(partial)
        whole = swap(jnp.broadcast_to(residual[None], (n_fas,) + residual.shape), "fas")
        (gradient,) = call(
            functools.partial(backward_kernel, cap, vox_rows),
            [flat_out],
            "svvv",
            [pltpu.VMEM((vox_rows, 2 * BV, LANES), bf16), table],
        )(meta, whole.reshape(image_rows, LANES), cp, at)
        bit = 1
        while bit < n_vox:
            gradient = gradient + lax.ppermute(
                gradient, "vox", [(i, i ^ bit) for i in range(n_vox)]
            )
            bit *= 2
        partial, projected, proj_sq = call(
            functools.partial(image_kernel, cap),
            [image_out, flat_out, ((8, LANES), f32, "v")],
            "svvvv",
            [table, acc],
        )(meta, gradient, weights, cp, a)
        image = collect(partial)
        image_sq = jnp.sum((image * image).reshape(-1, 4, LANES), axis=0)
        proj_sq = proj_sq[:4] + proj_sq[4:]
        sums = jnp.concatenate([image_sq, proj_sq], axis=0)
        sums = swap(jnp.broadcast_to(sums[None], (n_vox * n_fas, 8, LANES)), ("vox", "fas"))
        out = ((vox_rows, BV, LANES), f32, "v") if last else image_out
        partial, weights = call(
            functools.partial(update_kernel, cap, n_vox, last),
            [out, flat_out],
            "svvvvvv",
            [table, acc],
        )(meta, sums, projected, weights, sig, cp, a)
    final = partial.reshape(vox_rows, 2, n_fas, own, LANES)[..., :DIRS].transpose(2, 0, 3, 1, 4)
    final = swap(final.reshape(n_fas, vox_rows, own * 2 * DIRS), "fas")
    return (weights.reshape(-1), jnp.sum(final, axis=0))


def solution(mesh):
    placed = (
        P("vox", "fas"),
        P("fas"),
        P(("vox", "fas"), None),
        P(("vox", "fas")),
        P(("vox", "fas")),
        P(("vox", "fas"), None),
        P(("vox", "fas")),
        P(),
    )
    return jax.shard_map(
        functools.partial(local, mesh.shape["vox"], mesh.shape["fas"]),
        mesh=mesh,
        in_specs=placed,
        out_specs=(P("fas"), P("vox", "fas")),
        check_vma=False,
    )
```

time: 1830 us -> 497 us (0.27)
  waiting for transfers between devices: 840 us -> 91.6 us
  matrix products: 275 us -> 0 us
  blocking collectives: 442 us -> 222 us
  local copies, waits for them, and re-layouts: 207 us -> 10.4 us
  Pallas kernels: 0 us -> 138 us
  between operations: 22.6 us -> 1.92 us
  starting transfers between devices: 0.65 us -> 21.2 us
  other arithmetic: 31.2 us -> 11.5 us
    reduce_scatter x11 -> x0, waiting for transfers between devices: 687 us -> none  [collect(): lax.psum_scatter(partial_value, 'fas', scatter_dimension=1, tiled=True)]
    psum x10 -> x0, blocking collectives: 286 us -> none  [the longest x5 185 us: local(): image_sq = lax.psum(image_local, ('vox', 'fas'))]
    dot_general x32 -> x0, matrix products: 275 us -> none  [the longest x11 124 us: forward_accumulate(): jnp.einsum('kvj,kjd->kvd', scaled, atom_blk.astype(jnp.float32), precisio...]
    all_to_all x0 -> x16, blocking collectives: none -> 222 us  [swap(): return lax.all_to_all(x, axis, 0, 0)]
    all_gather x5 -> x0, blocking collectives: 157 us -> none  [local(): whole_rows = lax.all_gather(residual, 'fas', axis=1, tiled=True)]
    psum x5 -> x0, waiting for transfers between devices: 153 us -> none  [local(): lax.psum(backward_partial(whole_rows.reshape(vox_rows, BV, DIRS)), 'vox')]
    pallas_call x0 -> x17, Pallas kernels: none -> 138 us  [the longest x5 33.9 us: local(): call(functools.partial(backward_kernel, cap, vox_rows), [flat_out], 'svvv...]
    dot_general x11 -> x0, local copies, waits for them, and re-layouts: 94.4 us -> none  [forward_accumulate(): jnp.einsum('kvj,kjd->kvd', scaled, atom_blk.astype(jnp.float32), precisio...]
  transfers between devices with their start and end apart: 16 -> 15, of which waited for: 16 -> 15; matrix products, arithmetic and copies ran while one was open for 0% -> 0% of each run, Pallas kernels for 0% -> 0%
where the time goes in v1:
time: 497 us
  blocking collectives  222 us (45%)
  Pallas kernels  138 us (28%)
  waiting for transfers between devices  91.6 us (18%)
  starting transfers between devices  21.2 us (4%)
  other arithmetic  11.5 us (2%)
  local copies, waits for them, and re-layouts  10.4 us (2%)
    all_to_all x16, blocking collectives, swap(): return lax.all_to_all(x, axis, 0, 0)  222 us
    all_to_all x5, waiting for transfers between devices, swap(): return lax.all_to_all(x, axis, 0, 0)  57.3 us
    ppermute x10, waiting for transfers between devices, local(): lax.ppermute(gradient, 'vox', [(i, i ^ bit) for i in range(n_vox)])  34.4 us
    pallas_call x5, Pallas kernels, local(): call(functools.partial(backward_kernel, cap, vox_rows), [flat_out], 'svvv...  33.9 us
    pallas_call x5, Pallas kernels, local(): call(functools.partial(update_kernel, cap, n_vox, last), [out, flat_out],...  33.9 us
    pallas_call x5, Pallas kernels, local(): call(functools.partial(image_kernel, cap), [image_out, flat_out, ((8, LAN...  32.6 us
    pallas_call x1, Pallas kernels, local(): call(functools.partial(setup_kernel, vox_rows, fas_rows, cap), [((cap, BV...  31 us
    all_to_all x5, starting transfers between devices, swap(): return lax.all_to_all(x, axis, 0, 0)  20.5 us
  transfers between devices with their start and end apart: 15, of which 15 were waited for; matrix products, arithmetic and copies ran while one was open for 0% of the time, Pallas kernels for 0%

profile of v1, /device:TPU:0, one launch (start us, length us, event | category | flops | bytes accessed | tf_op | source)
XLA Modules:
  0.0 496.9 jit_solution(7908797032655074064)
XLA Ops:
  7.0 31.0 %shard_map.95 = (bf16[80,64,256]{2,1,0:T(8,128)(2,1)S(1)}, bf16[80,128,256]{2,1,0:T(8,128)(2,1)}, bf16[80,256,128]{2,1,0:T(8,128)(2,1)}, s32[512]{0:T(512)S(1)}) custom-call(s32[256]{0:T(256)S(1)} %copy-done.7, s32[256]{0:T(256)S(1)} %copy-done.8, s32[1]{0:T(128)S(6)} %copy.42.count_ref, bf16[256,32,128]{2,1,0:T(8,128)(2,1)S(1)} %bitcast.40, ...), custom_call_target="tpu_custom_call" | custom-call | tf_op jit(solution)/shard_map/pallas_call | solution.py:311
  38.0 6.5 %shard_map.96 = f32[768,128]{1,0:T(8,128)S(1)} custom-call(s32[512]{0:T(512)S(1)} %get-tuple-element.31.meta_ref, f32[256,128]{1,0:T(8,128)S(1)} %bitcast.47, f32[16,64,128]{2,1,0:T(8,128)S(1)} %bitcast.34, bf16[80,64,256]{2,1,0:T(8,128)(2,1)S(1)} %get-tuple-element.32.cp_ref, bf16[80,256,128]{2,1,0:T(8,128)(2,1)} %get-tuple-element.33.a_ref), custom_call_target="tpu_custom_call" | custom-call | tf_op jit(solution)/shard_map/pallas_call | solution.py:345
  44.5 18.8 %all_to_all.105 = f32[8,96,128]{2,1,0:T(8,128)} all-to-all(f32[8,96,128]{2,1,0:T(8,128)S(1)} %bitcast.46), channel_id=1, replica_groups=mesh['vox'=4,'fas'=8] {'fas'}, dimensions={0} | all-to-all | bytes 786432 | tf_op jit(solution)/shard_map/all_to_all | solution.py:338
  64.4 14.6 %all_to_all.106 = f32[8,96,128]{2,1,0:T(8,128)S(1)} all-to-all(f32[8,96,128]{2,1,0:T(8,128)S(1)} %broadcast_in_dim.23), channel_id=1, replica_groups=mesh['vox'=4,'fas'=8] {'fas'}, dimensions={0} | all-to-all | bytes 786432 | tf_op jit(solution)/shard_map/all_to_all | solution.py:338
  79.1 6.8 %shard_map.97 = f32[256,128]{1,0:T(8,128)S(1)} custom-call(s32[512]{0:T(512)S(1)} %get-tuple-element.31.meta_ref, f32[768,128]{1,0:T(8,128)S(1)} %bitcast.41, bf16[80,64,256]{2,1,0:T(8,128)(2,1)S(1)} %get-tuple-element.32.cp_ref, bf16[80,128,256]{2,1,0:T(8,128)(2,1)} %get-tuple-element.34.at_ref), custom_call_target="tpu_custom_call" | custom-call | tf_op jit(solution)/shard_map/pallas_call | solution.py:352
  87.4 5.5 %collective-permute-done.1 = f32[256,128]{1,0:T(8,128)S(1)} collective-permute-done((f32[256,128]{1,0:T(8,128)S(1)}, f32[256,128]{1,0:T(8,128)S(1)}, u32[]{:S(2)}, u32[]{:S(2)}) %collective-permute-start.1) | collective-permute-done | bytes 131104 | tf_op jit(solution)/shard_map/ppermute | solution.py:360
  92.9 6.5 %shard_map.98 = (f32[768,128]{1,0:T(8,128)S(1)}, f32[256,128]{1,0:T(8,128)S(1)}, f32[8,128]{1,0:T(8,128)S(1)}) custom-call(s32[512]{0:T(512)S(1)} %get-tuple-element.31.meta_ref, f32[256,128]{1,0:T(8,128)S(1)} %add.54.g_ref, f32[256,128]{1,0:T(8,128)S(1)} %bitcast.48, bf16[80,64,256]{2,1,0:T(8,128)(2,1)S(1)} %get-tuple-element.32.cp_ref, ...), custom_call_target="tpu_custom_call" | custom-call | tf_op jit(solution)/shard_map/pallas_call | solution.py:364
  100.2 4.1 all-to-all-start.2
  104.3 11.5 %all-to-all-done.2 = f32[8,96,128]{2,1,0:T(8,128)} async-done(((f32[8,96,128]{2,1,0:T(8,128)}), f32[8,96,128]{2,1,0:T(8,128)}, u32[]{:S(2)}, u32[]{:S(2)}) %all-to-all-start.2) | async-done | bytes 393248 | tf_op jit(solution)/shard_map/all_to_all | solution.py:338
  116.9 10.3 %all_to_all.107.sums_ref = f32[32,8,128]{2,1,0:T(8,128)S(1)} all-to-all(f32[32,8,128]{2,1,0:T(8,128)S(1)} %broadcast_in_dim.24), channel_id=1, replica_groups=mesh['vox'=4,'fas'=8] {'vox','fas'}, dimensions={0} | all-to-all | bytes 262144 | tf_op jit(solution)/shard_map/all_to_all | solution.py:338
  127.1 6.7 %shard_map.99 = (f32[768,128]{1,0:T(8,128)S(1)}, f32[256,128]{1,0:T(8,128)S(1)}) custom-call(s32[512]{0:T(512)S(1)} %get-tuple-element.31.meta_ref, f32[32,8,128]{2,1,0:T(8,128)S(1)} %all_to_all.107.sums_ref, f32[256,128]{1,0:T(8,128)S(1)} %get-tuple-element.37.p_ref, f32[256,128]{1,0:T(8,128)S(1)} %bitcast.49, f32[16,64,128]{2,1,0:T(8,128)S(1)} %bitcast.35, ...), custom_call_target="tpu_custom_call" | custom-call | tf_op jit(solution)/shard_map/pallas_call | solution.py:376
  133.8 15.7 %all_to_all.108 = f32[8,96,128]{2,1,0:T(8,128)} all-to-all(f32[8,96,128]{2,1,0:T(8,128)S(1)} %bitcast.59), channel_id=1, replica_groups=mesh['vox'=4,'fas'=8] {'fas'}, dimensions={0} | all-to-all | bytes 786432 | tf_op jit(solution)/shard_map/all_to_all | solution.py:338
  150.5 15.0 %all_to_all.109 = f32[8,96,128]{2,1,0:T(8,128)S(1)} all-to-all(f32[8,96,128]{2,1,0:T(8,128)S(1)} %broadcast_in_dim.25), channel_id=1, replica_groups=mesh['vox'=4,'fas'=8] {'fas'}, dimensions={0} | all-to-all | bytes 786432 | tf_op jit(solution)/shard_map/all_to_all | solution.py:338
  165.5 6.8 %shard_map.100 = f32[256,128]{1,0:T(8,128)S(1)} custom-call(s32[512]{0:T(512)S(1)} %get-tuple-element.31.meta_ref, f32[768,128]{1,0:T(8,128)S(1)} %bitcast.43, bf16[80,64,256]{2,1,0:T(8,128)(2,1)S(1)} %get-tuple-element.32.cp_ref, bf16[80,128,256]{2,1,0:T(8,128)(2,1)} %get-tuple-element.34.at_ref), custom_call_target="tpu_custom_call" | custom-call | tf_op jit(solution)/shard_map/pallas_call | solution.py:352
  173.9 5.5 %collective-permute-done.3 = f32[256,128]{1,0:T(8,128)S(1)} collective-permute-done((f32[256,128]{1,0:T(8,128)S(1)}, f32[256,128]{1,0:T(8,128)S(1)}, u32[]{:S(2)}, u32[]{:S(2)}) %collective-permute-start.3) | collective-permute-done | bytes 131104 | tf_op jit(solution)/shard_map/ppermute | solution.py:360
  179.4 6.5 %shard_map.101 = (f32[768,128]{1,0:T(8,128)S(1)}, f32[256,128]{1,0:T(8,128)S(1)}, f32[8,128]{1,0:T(8,128)S(1)}) custom-call(s32[512]{0:T(512)S(1)} %get-tuple-element.31.meta_ref, f32[256,128]{1,0:T(8,128)S(1)} %add.57.g_ref, f32[256,128]{1,0:T(8,128)S(1)} %get-tuple-element.39.w_ref, bf16[80,64,256]{2,1,0:T(8,128)(2,1)S(1)} %get-tuple-element.32.cp_ref, ...), custom_call_target="tpu_custom_call" | custom-call | tf_op jit(solution)/shard_map/pallas_call | solution.py:364
  186.7 4.1 all-to-all-start.6
  190.8 11.5 %all-to-all-done.6 = f32[8,96,128]{2,1,0:T(8,128)} async-done(((f32[8,96,128]{2,1,0:T(8,128)}), f32[8,96,128]{2,1,0:T(8,128)}, u32[]{:S(2)}, u32[]{:S(2)}) %all-to-all-start.6) | async-done | bytes 393248 | tf_op jit(solution)/shard_map/all_to_all | solution.py:338
  203.4 10.3 %all_to_all.110.sums_ref = f32[32,8,128]{2,1,0:T(8,128)S(1)} all-to-all(f32[32,8,128]{2,1,0:T(8,128)S(1)} %broadcast_in_dim.26), channel_id=1, replica_groups=mesh['vox'=4,'fas'=8] {'vox','fas'}, dimensions={0} | all-to-all | bytes 262144 | tf_op jit(solution)/shard_map/all_to_all | solution.py:338
  213.6 6.7 %shard_map.102 = (f32[768,128]{1,0:T(8,128)S(1)}, f32[256,128]{1,0:T(8,128)S(1)}) custom-call(s32[512]{0:T(512)S(1)} %get-tuple-element.31.meta_ref, f32[32,8,128]{2,1,0:T(8,128)S(1)} %all_to_all.110.sums_ref, f32[256,128]{1,0:T(8,128)S(1)} %get-tuple-element.42.p_ref, f32[256,128]{1,0:T(8,128)S(1)} %get-tuple-element.39.w_ref, f32[16,64,128]{2,1,0:T(8,128)S(1)} %bitcast.36, ...), custom_call_target="tpu_custom_call" | custom-call | tf_op jit(solution)/shard_map/pallas_call | solution.py:376
  220.3 15.7 %all_to_all.111 = f32[8,96,128]{2,1,0:T(8,128)} all-to-all(f32[8,96,128]{2,1,0:T(8,128)S(1)} %bitcast.56), channel_id=1, replica_groups=mesh['vox'=4,'fas'=8] {'fas'}, dimensions={0} | all-to-all | bytes 786432 | tf_op jit(solution)/shard_map/all_to_all | solution.py:338
  237.0 15.0 %all_to_all.112 = f32[8,96,128]{2,1,0:T(8,128)S(1)} all-to-all(f32[8,96,128]{2,1,0:T(8,128)S(1)} %broadcast_in_dim.27), channel_id=1, replica_groups=mesh['vox'=4,'fas'=8] {'fas'}, dimensions={0} | all-to-all | bytes 786432 | tf_op jit(solution)/shard_map/all_to_all | solution.py:338
  252.0 6.8 %shard_map.103 = f32[256,128]{1,0:T(8,128)S(1)} custom-call(s32[512]{0:T(512)S(1)} %get-tuple-element.31.meta_ref, f32[768,128]{1,0:T(8,128)S(1)} %bitcast.44, bf16[80,64,256]{2,1,0:T(8,128)(2,1)S(1)} %get-tuple-element.32.cp_ref, bf16[80,128,256]{2,1,0:T(8,128)(2,1)} %get-tuple-element.34.at_ref), custom_call_target="tpu_custom_call" | custom-call | tf_op jit(solution)/shard_map/pallas_call | solution.py:352
  260.3 5.5 %collective-permute-done.5 = f32[256,128]{1,0:T(8,128)S(1)} collective-permute-done((f32[256,128]{1,0:T(8,128)S(1)}, f32[256,128]{1,0:T(8,128)S(1)}, u32[]{:S(2)}, u32[]{:S(2)}) %collective-permute-start.5) | collective-permute-done | bytes 131104 | tf_op jit(solution)/shard_map/ppermute | solution.py:360
  265.9 6.5 %shard_map.104 = (f32[768,128]{1,0:T(8,128)S(1)}, f32[256,128]{1,0:T(8,128)S(1)}, f32[8,128]{1,0:T(8,128)S(1)}) custom-call(s32[512]{0:T(512)S(1)} %get-tuple-element.31.meta_ref, f32[256,128]{1,0:T(8,128)S(1)} %add.60.g_ref, f32[256,128]{1,0:T(8,128)S(1)} %get-tuple-element.44.w_ref, bf16[80,64,256]{2,1,0:T(8,128)(2,1)S(1)} %get-tuple-element.32.cp_ref, ...), custom_call_target="tpu_custom_call" | custom-call | tf_op jit(solution)/shard_map/pallas_call | solution.py:364
  273.2 4.1 all-to-all-start.10
  277.3 11.5 %all-to-all-done.10 = f32[8,96,128]{2,1,0:T(8,128)} async-done(((f32[8,96,128]{2,1,0:T(8,128)}), f32[8,96,128]{2,1,0:T(8,128)}, u32[]{:S(2)}, u32[]{:S(2)}) %all-to-all-start.10) | async-done | bytes 393248 | tf_op jit(solution)/shard_map/all_to_all | solution.py:338
  289.9 10.3 %all_to_all.113.sums_ref = f32[32,8,128]{2,1,0:T(8,128)S(1)} all-to-all(f32[32,8,128]{2,1,0:T(8,128)S(1)} %broadcast_in_dim.28), channel_id=1, replica_groups=mesh['vox'=4,'fas'=8] {'vox','fas'}, dimensions={0} | all-to-all | bytes 262144 | tf_op jit(solution)/shard_map/all_to_all | solution.py:338
  300.1 6.7 %shard_map.105 = (f32[768,128]{1,0:T(8,128)S(1)}, f32[256,128]{1,0:T(8,128)S(1)}) custom-call(s32[512]{0:T(512)S(1)} %get-tuple-element.31.meta_ref, f32[32,8,128]{2,1,0:T(8,128)S(1)} %all_to_all.113.sums_ref, f32[256,128]{1,0:T(8,128)S(1)} %get-tuple-element.47.p_ref, f32[256,128]{1,0:T(8,128)S(1)} %get-tuple-element.44.w_ref, f32[16,64,128]{2,1,0:T(8,128)S(1)} %bitcast.37, ...), custom_call_target="tpu_custom_call" | custom-call | tf_op jit(solution)/shard_map/pallas_call | solution.py:376
  306.8 15.7 %all_to_all.114 = f32[8,96,128]{2,1,0:T(8,128)} all-to-all(f32[8,96,128]{2,1,0:T(8,128)S(1)} %bitcast.57), channel_id=1, replica_groups=mesh['vox'=4,'fas'=8] {'fas'}, dimensions={0} | all-to-all | bytes 786432 | tf_op jit(solution)/shard_map/all_to_all | solution.py:338
  323.5 15.0 %all_to_all.115 = f32[8,96,128]{2,1,0:T(8,128)S(1)} all-to-all(f32[8,96,128]{2,1,0:T(8,128)S(1)} %broadcast_in_dim.29), channel_id=1, replica_groups=mesh['vox'=4,'fas'=8] {'fas'}, dimensions={0} | all-to-all | bytes 786432 | tf_op jit(solution)/shard_map/all_to_all | solution.py:338
  338.5 6.8 %shard_map.106 = f32[256,128]{1,0:T(8,128)S(1)} custom-call(s32[512]{0:T(512)S(1)} %get-tuple-element.31.meta_ref, f32[768,128]{1,0:T(8,128)S(1)} %bitcast.45, bf16[80,64,256]{2,1,0:T(8,128)(2,1)S(1)} %get-tuple-element.32.cp_ref, bf16[80,128,256]{2,1,0:T(8,128)(2,1)} %get-tuple-element.34.at_ref), custom_call_target="tpu_custom_call" | custom-call | tf_op jit(solution)/shard_map/pallas_call | solution.py:352
  346.8 5.5 %collective-permute-done.7 = f32[256,128]{1,0:T(8,128)S(1)} collective-permute-done((f32[256,128]{1,0:T(8,128)S(1)}, f32[256,128]{1,0:T(8,128)S(1)}, u32[]{:S(2)}, u32[]{:S(2)}) %collective-permute-start.7) | collective-permute-done | bytes 131104 | tf_op jit(solution)/shard_map/ppermute | solution.py:360
  352.4 6.5 %shard_map.107 = (f32[768,128]{1,0:T(8,128)S(1)}, f32[256,128]{1,0:T(8,128)S(1)}, f32[8,128]{1,0:T(8,128)S(1)}) custom-call(s32[512]{0:T(512)S(1)} %get-tuple-element.31.meta_ref, f32[256,128]{1,0:T(8,128)S(1)} %add.63.g_ref, f32[256,128]{1,0:T(8,128)S(1)} %get-tuple-element.49.w_ref, bf16[80,64,256]{2,1,0:T(8,128)(2,1)S(1)} %get-tuple-element.32.cp_ref, ...), custom_call_target="tpu_custom_call" | custom-call | tf_op jit(solution)/shard_map/pallas_call | solution.py:364
  359.7 4.1 all-to-all-start.14
  363.8 11.5 %all-to-all-done.14 = f32[8,96,128]{2,1,0:T(8,128)} async-done(((f32[8,96,128]{2,1,0:T(8,128)}), f32[8,96,128]{2,1,0:T(8,128)}, u32[]{:S(2)}, u32[]{:S(2)}) %all-to-all-start.14) | async-done | bytes 393248 | tf_op jit(solution)/shard_map/all_to_all | solution.py:338
  376.3 10.3 %all_to_all.116.sums_ref = f32[32,8,128]{2,1,0:T(8,128)S(1)} all-to-all(f32[32,8,128]{2,1,0:T(8,128)S(1)} %broadcast_in_dim.30), channel_id=1, replica_groups=mesh['vox'=4,'fas'=8] {'vox','fas'}, dimensions={0} | all-to-all | bytes 262144 | tf_op jit(solution)/shard_map/all_to_all | solution.py:338
  386.6 6.7 %shard_map.108 = (f32[768,128]{1,0:T(8,128)S(1)}, f32[256,128]{1,0:T(8,128)S(1)}) custom-call(s32[512]{0:T(512)S(1)} %get-tuple-element.31.meta_ref, f32[32,8,128]{2,1,0:T(8,128)S(1)} %all_to_all.116.sums_ref, f32[256,128]{1,0:T(8,128)S(1)} %get-tuple-element.52.p_ref, f32[256,128]{1,0:T(8,128)S(1)} %get-tuple-element.49.w_ref, f32[16,64,128]{2,1,0:T(8,128)S(1)} %bitcast.38, ...), custom_call_target="tpu_custom_call" | custom-call | tf_op jit(solution)/shard_map/pallas_call | solution.py:376
  393.3 15.7 %all_to_all.117 = f32[8,96,128]{2,1,0:T(8,128)} all-to-all(f32[8,96,128]{2,1,0:T(8,128)S(1)} %bitcast.58), channel_id=1, replica_groups=mesh['vox'=4,'fas'=8] {'fas'}, dimensions={0} | all-to-all | bytes 786432 | tf_op jit(solution)/shard_map/all_to_all | solution.py:338
  410.0 15.0 %all_to_all.118 = f32[8,96,128]{2,1,0:T(8,128)S(1)} all-to-all(f32[8,96,128]{2,1,0:T(8,128)S(1)} %broadcast_in_dim.31), channel_id=1, replica_groups=mesh['vox'=4,'fas'=8] {'fas'}, dimensions={0} | all-to-all | bytes 786432 | tf_op jit(solution)/shard_map/all_to_all | solution.py:338
  425.0 6.8 %shard_map.109 = f32[256,128]{1,0:T(8,128)S(1)} custom-call(s32[512]{0:T(512)S(1)} %get-tuple-element.31.meta_ref, f32[768,128]{1,0:T(8,128)S(1)} %bitcast.42, bf16[80,64,256]{2,1,0:T(8,128)(2,1)S(1)} %get-tuple-element.32.cp_ref, bf16[80,128,256]{2,1,0:T(8,128)(2,1)} %get-tuple-element.34.at_ref), custom_call_target="tpu_custom_call" | custom-call | tf_op jit(solution)/shard_map/pallas_call | solution.py:352
  433.3 5.5 %collective-permute-done.9 = f32[256,128]{1,0:T(8,128)S(1)} collective-permute-done((f32[256,128]{1,0:T(8,128)S(1)}, f32[256,128]{1,0:T(8,128)S(1)}, u32[]{:S(2)}, u32[]{:S(2)}) %collective-permute-start.9) | collective-permute-done | bytes 131104 | tf_op jit(solution)/shard_map/ppermute | solution.py:360
  438.9 6.5 %shard_map.110 = (f32[768,128]{1,0:T(8,128)S(1)}, f32[256,128]{1,0:T(8,128)S(1)}, f32[8,128]{1,0:T(8,128)S(1)}) custom-call(s32[512]{0:T(512)S(1)} %get-tuple-element.31.meta_ref, f32[256,128]{1,0:T(8,128)S(1)} %add.66.g_ref, f32[256,128]{1,0:T(8,128)S(1)} %get-tuple-element.54.w_ref, bf16[80,64,256]{2,1,0:T(8,128)(2,1)S(1)} %get-tuple-element.32.cp_ref, ...), custom_call_target="tpu_custom_call" | custom-call | tf_op jit(solution)/shard_map/pallas_call | solution.py:364
  446.2 4.1 all-to-all-start.18
  450.3 11.5 %all-to-all-done.18 = f32[8,96,128]{2,1,0:T(8,128)} async-done(((f32[8,96,128]{2,1,0:T(8,128)}), f32[8,96,128]{2,1,0:T(8,128)}, u32[]{:S(2)}, u32[]{:S(2)}) %all-to-all-start.18) | async-done | bytes 393248 | tf_op jit(solution)/shard_map/all_to_all | solution.py:338
  462.8 10.3 %all_to_all.119.sums_ref = f32[32,8,128]{2,1,0:T(8,128)S(1)} all-to-all(f32[32,8,128]{2,1,0:T(8,128)S(1)} %broadcast_in_dim.32), channel_id=1, replica_groups=mesh['vox'=4,'fas'=8] {'vox','fas'}, dimensions={0} | all-to-all | bytes 262144 | tf_op jit(solution)/shard_map/all_to_all | solution.py:338
  473.1 7.2 %shard_map.111 = (f32[16,64,128]{2,1,0:T(8,128)S(1)}, f32[256,128]{1,0:T(8,128)}) custom-call(s32[512]{0:T(512)S(1)} %get-tuple-element.31.meta_ref, f32[32,8,128]{2,1,0:T(8,128)S(1)} %all_to_all.119.sums_ref, f32[256,128]{1,0:T(8,128)S(1)} %get-tuple-element.57.p_ref, f32[256,128]{1,0:T(8,128)S(1)} %get-tuple-element.54.w_ref, f32[16,64,128]{2,1,0:T(8,128)S(1)} %bitcast.39, ...), custom_call_target="tpu_custom_call" | custom-call | tf_op jit(solution)/shard_map/pallas_call | solution.py:376
  481.3 15.0 %all_to_all.120 = f32[8,16,768]{2,1,0:T(8,128)S(1)} all-to-all(f32[8,16,768]{2,1,0:T(8,128)S(1)} %reshape.114), channel_id=1, replica_groups=mesh['vox'=4,'fas'=8] {'fas'}, dimensions={0} | all-to-all | bytes 786432 | tf_op jit(solution)/shard_map/all_to_all | solution.py:338
  (101 shorter events, 29.2 us)
Async XLA Ops:
  0.6 3.6 copy-start.10
  0.6 4.4 copy-start.11
  0.7 4.6 copy-start.9
  0.7 4.7 copy-start.7
  0.7 4.7 copy-start.8
  4.2 33.8 %copy-start.1 = (f32[32768]{0:T(1024)S(1)}, f32[32768]{0:T(1024)}, u32[]{:S(2)}) copy-start(f32[32768]{0:T(1024)} %param.9) | copy-start | bytes 393220
  5.4 1.6 copy-start
  85.8 1.4 collective-permute-start
  87.3 5.6 %collective-permute-start.1 = (f32[256,128]{1,0:T(8,128)S(1)}, f32[256,128]{1,0:T(8,128)S(1)}, u32[]{:S(2)}, u32[]{:S(2)}) collective-permute-start(f32[256,128]{1,0:T(8,128)S(1)} %add.53), channel_id=1, source_target_pairs={{0,16},{8,24},{16,0},{24,8},{1,17},{9,25},{17,1},{25,9},{2,18},{10... | collective-permute-start | bytes 393224 | tf_op jit(solution)/shard_map/ppermute | solution.py:360
  99.4 0.8 copy-start.2
  100.2 15.6 %all-to-all-start.2 = ((f32[8,96,128]{2,1,0:T(8,128)}), f32[8,96,128]{2,1,0:T(8,128)}, u32[]{:S(2)}, u32[]{:S(2)}) async-start(f32[8,96,128]{2,1,0:T(8,128)} %bitcast.51), calls=%async_computation.2 | async-start | bytes 786432 | tf_op jit(solution)/shard_map/all_to_all | solution.py:338
  172.3 1.4 collective-permute-start.2
  173.8 5.6 %collective-permute-start.3 = (f32[256,128]{1,0:T(8,128)S(1)}, f32[256,128]{1,0:T(8,128)S(1)}, u32[]{:S(2)}, u32[]{:S(2)}) collective-permute-start(f32[256,128]{1,0:T(8,128)S(1)} %add.56), channel_id=1, source_target_pairs={{0,16},{8,24},{16,0},{24,8},{1,17},{9,25},{17,1},{25,9},{2,18},{10... | collective-permute-start | bytes 393224 | tf_op jit(solution)/shard_map/ppermute | solution.py:360
  185.9 0.8 copy-start.3
  186.7 15.6 %all-to-all-start.6 = ((f32[8,96,128]{2,1,0:T(8,128)}), f32[8,96,128]{2,1,0:T(8,128)}, u32[]{:S(2)}, u32[]{:S(2)}) async-start(f32[8,96,128]{2,1,0:T(8,128)} %bitcast.52), calls=%async_computation.6 | async-start | bytes 786432 | tf_op jit(solution)/shard_map/all_to_all | solution.py:338
  258.8 1.4 collective-permute-start.4
  260.3 5.6 %collective-permute-start.5 = (f32[256,128]{1,0:T(8,128)S(1)}, f32[256,128]{1,0:T(8,128)S(1)}, u32[]{:S(2)}, u32[]{:S(2)}) collective-permute-start(f32[256,128]{1,0:T(8,128)S(1)} %add.59), channel_id=1, source_target_pairs={{0,16},{8,24},{16,0},{24,8},{1,17},{9,25},{17,1},{25,9},{2,18},{10... | collective-permute-start | bytes 393224 | tf_op jit(solution)/shard_map/ppermute | solution.py:360
  272.4 0.8 copy-start.4
  273.2 15.6 %all-to-all-start.10 = ((f32[8,96,128]{2,1,0:T(8,128)}), f32[8,96,128]{2,1,0:T(8,128)}, u32[]{:S(2)}, u32[]{:S(2)}) async-start(f32[8,96,128]{2,1,0:T(8,128)} %bitcast.53), calls=%async_computation.10 | async-start | bytes 786432 | tf_op jit(solution)/shard_map/all_to_all | solution.py:338
  345.3 1.4 collective-permute-start.6
  346.8 5.6 %collective-permute-start.7 = (f32[256,128]{1,0:T(8,128)S(1)}, f32[256,128]{1,0:T(8,128)S(1)}, u32[]{:S(2)}, u32[]{:S(2)}) collective-permute-start(f32[256,128]{1,0:T(8,128)S(1)} %add.62), channel_id=1, source_target_pairs={{0,16},{8,24},{16,0},{24,8},{1,17},{9,25},{17,1},{25,9},{2,18},{10... | collective-permute-start | bytes 393224 | tf_op jit(solution)/shard_map/ppermute | solution.py:360
  358.9 0.8 copy-start.5
  359.7 15.6 %all-to-all-start.14 = ((f32[8,96,128]{2,1,0:T(8,128)}), f32[8,96,128]{2,1,0:T(8,128)}, u32[]{:S(2)}, u32[]{:S(2)}) async-start(f32[8,96,128]{2,1,0:T(8,128)} %bitcast.54), calls=%async_computation.14 | async-start | bytes 786432 | tf_op jit(solution)/shard_map/all_to_all | solution.py:338
  431.8 1.4 collective-permute-start.8
  433.3 5.6 %collective-permute-start.9 = (f32[256,128]{1,0:T(8,128)S(1)}, f32[256,128]{1,0:T(8,128)S(1)}, u32[]{:S(2)}, u32[]{:S(2)}) collective-permute-start(f32[256,128]{1,0:T(8,128)S(1)} %add.65), channel_id=1, source_target_pairs={{0,16},{8,24},{16,0},{24,8},{1,17},{9,25},{17,1},{25,9},{2,18},{10... | collective-permute-start | bytes 393224 | tf_op jit(solution)/shard_map/ppermute | solution.py:360
  445.4 0.8 copy-start.6
  446.2 15.6 %all-to-all-start.18 = ((f32[8,96,128]{2,1,0:T(8,128)}), f32[8,96,128]{2,1,0:T(8,128)}, u32[]{:S(2)}, u32[]{:S(2)}) async-start(f32[8,96,128]{2,1,0:T(8,128)} %bitcast.55), calls=%async_computation.18 | async-start | bytes 786432 | tf_op jit(solution)/shard_map/all_to_all | solution.py:338
